TPU v7x, 128 devices: a whole 4x4x4 slice. The times are simulated.
128 devices in a mesh: row: 8 (over y_lo, x), col: 16 (over y_hi, z, core).
Axes of the slice: x: 4, y: 4 (y_hi: 2, y_lo: 2; y = y_hi * 2 + y_lo), z: 4, core: 2. Of those that a mesh axis runs over, the one named last changes fastest.
Arguments:
- spectra: float32 [2, 4, 30, 16, 512], P(None, None, None, 'col', 'row'), may hold values from -500 to 500
- counts: int32 [16, 512], P('col', 'row'), may hold values from 1 to 30
Outputs:
- stacks: float32 [16, 512, 9, 2, 4, 512], P('col', 'row')
All inputs are finite; a program needn't handle non-finite values.
Results may differ from a plain program's by a relative error of at most 0.004.
Values may be sent and summed in bfloat16 or wider, within the bound.
A program may use at most 64 MiB of HBM per device.

v0:
```python
import functools

import jax
import jax.numpy as jnp
from jax import lax
from jax.experimental import pallas as pl
from jax.experimental.pallas import tpu as pltpu
from jax.sharding import PartitionSpec as P

MESH = pl.DeviceIdType.MESH
BINS = 4
SEGS = 30
USED = 2 * BINS * SEGS
COLS = 256
WIDTH = 64
HALF = 32
SHARED = 14
HOPS = 9
SEL = 16


def gather_kernel(spec_in, cnt_in, gl, gh, lhs, rci, spec, cnt, own, ssem, rsem, lsem):
    fetch = (
        pltpu.make_async_copy(spec_in, spec, lsem.at[1]),
        pltpu.make_async_copy(cnt_in, cnt, lsem.at[2]),
    )
    for copy in fetch:
        copy.start()
    r, d = lax.axis_index("row"), lax.axis_index("col")
    x, ylo = r % 4, r // 4
    c, q = d % 2, d // 2
    z, yhi = q % 4, q // 4

    def dev(x_, ylo_, q_, c_):
        return (ylo_ * 4 + x_, q_ * 2 + c_)

    sibling = dev(x, ylo, q, 1 - c)
    across = 1 - ylo

    steps = (2, 1, 3)
    y_steps = ((0, 1), (1, 1), (1, 0))

    def along_x(i):
        return dev((x + i) % 4, ylo, q, c)

    def along_y(four_on, rel):
        return dev(x, across if rel else ylo, (q + 4 * four_on) % 8, c)

    def along_z(e):
        return dev(x, ylo, yhi * 4 + (z + e) % 4, c)

    barrier = pltpu.get_barrier_semaphore()
    sources = [along_x(i) for i in steps] + [along_y(*at) for at in y_steps]
    sources += [along_z(e) for e in steps] + [sibling]
    for source in sources:
        pl.semaphore_signal(barrier, inc=1, device_id=source, device_id_type=MESH)

    for copy in fetch:
        copy.wait()
    raw = spec[...]
    power = jnp.sum(raw * raw, axis=0, keepdims=True) / float(USED)
    row = lax.broadcasted_iota(jnp.int32, (USED, WIDTH), 0)
    group = jnp.zeros((USED, WIDTH), jnp.int32)
    for n in range(1, 2 * BINS):
        group = group + (row >= n * SEGS).astype(jnp.int32)
    valid = (row - SEGS * group < cnt[...]).astype(jnp.float32)
    white = raw * lax.rsqrt(power + 1e-6) * valid
    white = white.astype(jnp.bfloat16).astype(jnp.float32)
    count = cnt[...].astype(jnp.float32)
    pad = jnp.zeros((COLS - USED - 8, WIDTH), jnp.float32)
    first = lax.broadcasted_iota(jnp.int32, (8, WIDTH), 0) == 0
    tail = jnp.where(first, count, 0.0)
    straight = jnp.concatenate([white, tail, pad], axis=0).T
    own[...] = straight.astype(jnp.bfloat16)

    def plan(src, dst, device, send, recv):
        return pltpu.make_async_remote_copy(
            src_ref=src,
            dst_ref=dst,
            send_sem=ssem.at[send],
            recv_sem=rsem.at[recv],
            device_id=device,
            device_id_type=MESH,
        )

    def remote(src, dst, device, send, recv):
        copy = plan(src, dst, device, send, recv)
        copy.start()
        return copy

    def settle(region, sem):
        pltpu.make_async_copy(region, region, sem).wait()

    every = slice(None)
    own_lo, own_hi = own.at[pl.ds(0, HALF)], own.at[pl.ds(HALF, HALF)]
    pl.semaphore_wait(barrier, len(sources))
    for i in steps:
        remote(own_hi, gh.at[0, ylo, x], along_x(i), 0, 0)
    for four_on, rel in y_steps:
        remote(own_lo, gl.at[four_on, ylo, x], along_y(four_on, rel), 1, 1)
    local = [
        pltpu.make_async_copy(own_lo, gl.at[0, ylo, x], lsem.at[0]),
        pltpu.make_async_copy(own_hi, gh.at[0, ylo, x], lsem.at[3]),
    ]
    for copy in local:
        copy.start()

    for copy in local:
        copy.wait()

    def share(half, index, to, send):
        remote(half.at[index], half.at[to], sibling, send, SHARED + send)

    def share_end(half, send):
        share(half, 1 - c, 8 - 3 * c, send)

    def x_copies(blocks, send, recv):
        column = gl.at[blocks, :, x]
        return {i: remote(column, column, along_x(i), send, recv + i) for i in steps}

    taken = {e: jnp.where((z + 4 - e) % 4 > z, 1, 0) for e in (3, 2, 1)}

    settle(gh.at[0, 0, pl.ds(0, 3)], rsem.at[0])
    for four_on, rel in y_steps:
        remote(gh.at[0, ylo], gh.at[four_on, ylo], along_y(four_on, rel), 4, 2 + 10 * four_on)
    settle(gl.at[0, 0, pl.ds(0, 3)], rsem.at[1])
    for e in taken:
        remote(gl.at[taken[e], :, x], gl.at[1 + e, :, x], along_z(-e), 5, 3)
    z_copies = {
        e: plan(gh.at[taken[e]], gh.at[1 + e], along_z(-e), 7, 12 + e) for e in taken
    }

    settle(gh.at[0, 0], rsem.at[2])
    for e in taken:
        pl.when(taken[e] == 0)(z_copies[e].start)
    near = x_copies(pl.ds(0, 2), 6, 4)
    settle(gh.at[0], rsem.at[12])
    for e in taken:
        pl.when(taken[e] == 1)(z_copies[e].start)
    share_end(gh, 2)
    settle(gl.at[0, pl.ds(0, 2), pl.ds(0, 3)], rsem.at[3])
    rest = pl.ds(2, 3)
    beyond = x_copies(rest, 8, 8)
    for i in steps:
        near[i].wait_recv()
    share_end(gl, 3)

    swapped = jnp.concatenate(
        [white[USED // 2 :], -white[: USED // 2], jnp.zeros((COLS - USED, WIDTH), jnp.float32)],
        axis=0,
    ).T
    shape = (WIDTH, 8, COLS)
    sub = lax.broadcasted_iota(jnp.int32, (8, COLS), 0)
    lane = lax.broadcasted_iota(jnp.int32, (8, COLS), 1)
    low = (sub % BINS) * SEGS
    here = ((lane >= low) & (lane < low + SEGS)) | (
        (lane >= low + USED // 2) & (lane < low + USED // 2 + SEGS)
    )
    one = jnp.broadcast_to(straight[:, None, :], shape)
    two = jnp.broadcast_to(swapped[:, None, :], shape)
    sel = lax.broadcasted_iota(jnp.int32, (SEL, COLS), 1) == USED
    for odd in (0, 1):
        pick = jnp.where(((sub < BINS) == (odd == 0))[None], one, two)
        pick = jnp.where(here[None], pick, 0.0)
        lhs[odd, :SEL, :] = sel.astype(jnp.float32).astype(jnp.bfloat16)
        lhs[odd, SEL:, :] = pick.reshape(WIDTH * 8, COLS).astype(jnp.bfloat16)
    mine = jnp.broadcast_to(1.0 / straight[:, USED : USED + 1], (WIDTH, 128))
    rci[...] = jnp.broadcast_to(mine[:, None, :], (WIDTH, 8, 128)).reshape(WIDTH * 8, 128)

    for e in taken:
        z_copies[e].wait_recv()
        share(gh, 1 + e, 4 + e + c, 2)
    for i in (0,) + steps:
        if i:
            beyond[i].wait_recv()
        at = (x + 4 - i) % 4
        share(gl, (rest, every, at), (pl.ds(5 + c, 3), every, at), 3)

    settle(gh.at[pl.ds(5, 4)], rsem.at[SHARED + 2])
    settle(gl.at[pl.ds(5, 4)], rsem.at[SHARED + 3])
    settle(gh.at[0, 0, pl.ds(0, 3)], ssem.at[0])
    settle(gl.at[0, 0, pl.ds(0, 3)], ssem.at[1])
    settle(gh.at[pl.ds(5, 4)], ssem.at[2])
    settle(gl.at[pl.ds(5, 4)], ssem.at[3])
    settle(gh.at[pl.ds(0, 3), 0], ssem.at[4])
    settle(gl.at[0, pl.ds(0, 2), pl.ds(0, 3)], ssem.at[5])
    settle(gl.at[pl.ds(0, 2), :, pl.ds(0, 3)], ssem.at[6])
    settle(gh.at[pl.ds(0, 3)], ssem.at[7])
    settle(gl.at[pl.ds(0, 3), :, pl.ds(0, 3)], ssem.at[8])


def stack_kernel(gl, gh, lhs, rci, out, stage, sems):
    mine = rci[...]

    def held(k):
        even = jnp.where(k == 0, 0, jnp.where(k == 8, 1, 1 + k // 2))
        return jnp.where(k % 2 == 0, even, 5 + k // 2)

    def to_out(k):
        return pltpu.make_async_copy(stage.at[k], out.at[:, k], sems.at[k])

    @pl.loop(0, HOPS, unroll=3)
    def _(k):
        def tiles(odd):
            pieces = [(n, at) for n in (0, 1) for at in (2 * odd, 2 * odd + 1)]
            right = [half[(held(k),) + piece] for piece in pieces for half in (gl, gh)]
            result = lax.dot_general(
                lhs[odd],
                jnp.concatenate(right, axis=0),
                (((1,), (1,)), ((), ())),
                preferred_element_type=jnp.float32,
            )
            recip = 1.0 / result[0:1]
            halves = (slice(0, 128), slice(128, 256))
            return [
                (result[SEL:, lanes] * jnp.maximum(mine, recip[:, lanes])).reshape(WIDTH, 8, 128)
                for lanes in halves
            ]

        lower = lax.broadcasted_iota(jnp.int32, (WIDTH, 8, 128), 1) < BINS
        for n, (even, odd) in enumerate(zip(tiles(0), tiles(1))):
            rows = pl.ds(8 * n, 8)
            stage[k, :, 0, rows] = jnp.where(lower, even, odd)
            stage[k, :, 1, rows] = pltpu.roll(jnp.where(lower, odd, even), BINS, 1)
        to_out(k).start()

    @pl.loop(0, HOPS)
    def _(k):
        to_out(k).wait()


def per_device(spectra, counts):
    spec = spectra.reshape(USED, WIDTH)
    vmem = pl.BlockSpec(memory_space=pltpu.VMEM)
    hbm = pl.BlockSpec(memory_space=pltpu.HBM)
    gl, gh, lhs, rci = pl.pallas_call(
        gather_kernel,
        name="whiten_gather",
        out_shape=(
            jax.ShapeDtypeStruct((HOPS, 2, 4, HALF, COLS), jnp.bfloat16),
            jax.ShapeDtypeStruct((HOPS, 2, 4, HALF, COLS), jnp.bfloat16),
            jax.ShapeDtypeStruct((2, SEL + WIDTH * 8, COLS), jnp.bfloat16),
            jax.ShapeDtypeStruct((WIDTH * 8, 128), jnp.float32),
        ),
        in_specs=[hbm, hbm],
        out_specs=(vmem,) * 4,
        scratch_shapes=[
            pltpu.VMEM((USED, WIDTH), jnp.float32),
            pltpu.VMEM((1, WIDTH), jnp.int32),
            pltpu.VMEM((WIDTH, COLS), jnp.bfloat16),
            pltpu.SemaphoreType.DMA((9,)),
            pltpu.SemaphoreType.DMA((SHARED + 4,)),
            pltpu.SemaphoreType.DMA((4,)),
        ],
        compiler_params=pltpu.CompilerParams(
            collective_id=0, has_side_effects=True, vmem_limit_bytes=16 * 2**20
        ),
    )(*(pltpu.with_memory_space_constraint(a, pltpu.HBM) for a in (spec, counts)))
    out = pl.pallas_call(
        stack_kernel,
        name="stack",
        out_shape=jax.ShapeDtypeStruct((WIDTH, HOPS, 2, 4 * BINS, 128), jnp.float32),
        in_specs=[vmem] * 4,
        out_specs=hbm,
        scratch_shapes=[
            pltpu.VMEM((HOPS, WIDTH, 2, 4 * BINS, 128), jnp.float32),
            pltpu.SemaphoreType.DMA((HOPS,)),
        ],
        compiler_params=pltpu.CompilerParams(vmem_limit_bytes=24 * 2**20),
        cost_estimate=pl.CostEstimate(
            flops=2 * (SEL + WIDTH * 8) * COLS * 512 * HOPS,
            bytes_accessed=HOPS * 512 * (COLS * 2 + WIDTH * 8 * 4),
            transcendentals=0,
        ),
    )(gl, gh, lhs, rci)
    out = out.reshape(WIDTH, HOPS, 2, 4, BINS, 128).swapaxes(3, 4)
    return out.reshape(1, WIDTH, HOPS, 2, BINS, 512)


def solution(mesh):
    return jax.shard_map(
        per_device,
        mesh=mesh,
        in_specs=(P(None, None, None, "col", "row"), P("col", "row")),
        out_specs=P("col", "row", None, None, None, None),
        check_vma=False,
    )
```

profile of v0, /device:TPU:1, one launch (start us, length us, event | category | flops | bytes accessed | tf_op | source)
XLA Modules:
  0.0 27.4 jit_solution(13841262544102739820)
XLA Ops:
  0.0 23.4 %whiten_gather.1 = (bf16[9,2,4,32,256]{4,3,2,1,0:T(8,128)(2,1)S(1)}, bf16[9,2,4,32,256]{4,3,2,1,0:T(8,128)(2,1)S(1)}, bf16[2,528,256]{2,1,0:T(8,128)(2,1)S(1)}, f32[512,128]{1,0:T(8,128)S(1)}) custom-call(f32[240,64]{1,0:T(8,128)} %bitcast.6, s32[1,64]{1,0:T(1,128)} %cnt_in.1), custom_call_target="tpu_custom_call" | custom-call | tf_op jit(solution)/shard_map/whiten_gather/pallas_call | solution.py:236
  23.4 4.1 %stack.1 = f32[64,9,2,16,128]{4,3,2,1,0:T(8,128)} custom-call(bf16[9,2,4,32,256]{4,3,2,1,0:T(8,128)(2,1)S(1)} %get-tuple-element.9.gl, bf16[9,2,4,32,256]{4,3,2,1,0:T(8,128)(2,1)S(1)} %get-tuple-element.10.gh, bf16[2,528,256]{2,1,0:T(8,128)(2,1)S(1)} %get-tuple-element.11.lhs, f32[512,128]{1,0:T(8,128)S(1)} %get-tuple-element.12.rci), custom_call_target="tpu_custom_call" | custom-call | flops 1245708288 | bytes 11796480 | tf_op jit(solution)/shard_map/stack/pallas_call | solution.py:259
where the time goes:
time: 27.6 us; the launch traced here: 27.4 us
  Pallas kernels  27.4 us (99%)
    pallas_call x1, Pallas kernels, per_device(): pl.pallas_call(gather_kernel, name='whiten_gather', out_shape=(jax.ShapeD...  23.4 us
    pallas_call x1, Pallas kernels, per_device(): pl.pallas_call(stack_kernel, name='stack', out_shape=jax.ShapeDtypeStruct...  4.06 us

commit v1 on v0

--- a/solution.py
+++ b/solution.py
@@ -19,7 +19,33 @@
 SEL = 16
 
 
-def gather_kernel(spec_in, cnt_in, gl, gh, lhs, rci, spec, cnt, own, ssem, rsem, lsem):
+def one_hop(gl, gh, held, lhs, rci, to):
+    mine = rci[...]
+
+    def tiles(odd):
+        pieces = [(held, n, at) for n in (0, 1) for at in (2 * odd, 2 * odd + 1)]
+        right = [half[piece] for piece in pieces for half in (gl, gh)]
+        result = lax.dot_general(
+            lhs[odd],
+            jnp.concatenate(right, axis=0),
+            (((1,), (1,)), ((), ())),
+            preferred_element_type=jnp.float32,
+        )
+        recip = 1.0 / result[0:1]
+        halves = (slice(0, 128), slice(128, 256))
+        return [
+            (result[SEL:, lanes] * jnp.maximum(mine, recip[:, lanes])).reshape(WIDTH, 8, 128)
+            for lanes in halves
+        ]
+
+    lower = lax.broadcasted_iota(jnp.int32, (WIDTH, 8, 128), 1) < BINS
+    for n, (even, odd) in enumerate(zip(tiles(0), tiles(1))):
+        rows = pl.ds(8 * n, 8)
+        to[:, 0, rows] = jnp.where(lower, even, odd)
+        to[:, 1, rows] = pltpu.roll(jnp.where(lower, odd, even), BINS, 1)
+
+
+def gather_kernel(spec_in, cnt_in, gl, gh, lhs, rci, ready, spec, cnt, own, ssem, rsem, lsem):
     fetch = (
         pltpu.make_async_copy(spec_in, spec, lsem.at[1]),
         pltpu.make_async_copy(cnt_in, cnt, lsem.at[2]),
@@ -104,46 +130,6 @@
     ]
     for copy in local:
         copy.start()
-
-    for copy in local:
-        copy.wait()
-
-    def share(half, index, to, send):
-        remote(half.at[index], half.at[to], sibling, send, SHARED + send)
-
-    def share_end(half, send):
-        share(half, 1 - c, 8 - 3 * c, send)
-
-    def x_copies(blocks, send, recv):
-        column = gl.at[blocks, :, x]
-        return {i: remote(column, column, along_x(i), send, recv + i) for i in steps}
-
-    taken = {e: jnp.where((z + 4 - e) % 4 > z, 1, 0) for e in (3, 2, 1)}
-
-    settle(gh.at[0, 0, pl.ds(0, 3)], rsem.at[0])
-    for four_on, rel in y_steps:
-        remote(gh.at[0, ylo], gh.at[four_on, ylo], along_y(four_on, rel), 4, 2 + 10 * four_on)
-    settle(gl.at[0, 0, pl.ds(0, 3)], rsem.at[1])
-    for e in taken:
-        remote(gl.at[taken[e], :, x], gl.at[1 + e, :, x], along_z(-e), 5, 3)
-    z_copies = {
-        e: plan(gh.at[taken[e]], gh.at[1 + e], along_z(-e), 7, 12 + e) for e in taken
-    }
-
-    settle(gh.at[0, 0], rsem.at[2])
-    for e in taken:
-        pl.when(taken[e] == 0)(z_copies[e].start)
-    near = x_copies(pl.ds(0, 2), 6, 4)
-    settle(gh.at[0], rsem.at[12])
-    for e in taken:
-        pl.when(taken[e] == 1)(z_copies[e].start)
-    share_end(gh, 2)
-    settle(gl.at[0, pl.ds(0, 2), pl.ds(0, 3)], rsem.at[3])
-    rest = pl.ds(2, 3)
-    beyond = x_copies(rest, 8, 8)
-    for i in steps:
-        near[i].wait_recv()
-    share_end(gl, 3)
 
     swapped = jnp.concatenate(
         [white[USED // 2 :], -white[: USED // 2], jnp.zeros((COLS - USED, WIDTH), jnp.float32)],
@@ -167,6 +153,49 @@
     mine = jnp.broadcast_to(1.0 / straight[:, USED : USED + 1], (WIDTH, 128))
     rci[...] = jnp.broadcast_to(mine[:, None, :], (WIDTH, 8, 128)).reshape(WIDTH * 8, 128)
 
+    for copy in local:
+        copy.wait()
+
+    def share(half, index, to, send):
+        remote(half.at[index], half.at[to], sibling, send, SHARED + send)
+
+    def share_end(half, send):
+        share(half, 1 - c, 8 - 3 * c, send)
+
+    def x_copies(blocks, send, recv):
+        column = gl.at[blocks, :, x]
+        return {i: remote(column, column, along_x(i), send, recv + i) for i in steps}
+
+    taken = {e: jnp.where((z + 4 - e) % 4 > z, 1, 0) for e in (3, 2, 1)}
+
+    settle(gh.at[0, 0, pl.ds(0, 3)], rsem.at[0])
+    for four_on, rel in y_steps:
+        remote(gh.at[0, ylo], gh.at[four_on, ylo], along_y(four_on, rel), 4, 2 + 10 * four_on)
+    settle(gl.at[0, 0, pl.ds(0, 3)], rsem.at[1])
+    for e in taken:
+        remote(gl.at[taken[e], :, x], gl.at[1 + e, :, x], along_z(-e), 5, 3)
+    z_copies = {
+        e: plan(gh.at[taken[e]], gh.at[1 + e], along_z(-e), 7, 12 + e) for e in taken
+    }
+
+    settle(gh.at[0, 0], rsem.at[2])
+    for e in taken:
+        pl.when(taken[e] == 0)(z_copies[e].start)
+    near = x_copies(pl.ds(0, 2), 6, 4)
+    settle(gh.at[0], rsem.at[12])
+    for e in taken:
+        pl.when(taken[e] == 1)(z_copies[e].start)
+    share_end(gh, 2)
+    settle(gl.at[0, pl.ds(0, 2), pl.ds(0, 3)], rsem.at[3])
+    rest = pl.ds(2, 3)
+    beyond = x_copies(rest, 8, 8)
+    for i in steps:
+        near[i].wait_recv()
+    share_end(gl, 3)
+
+    for n in (0, 1):
+        one_hop(gl, gh, n, lhs, rci, ready.at[n])
+
     for e in taken:
         z_copies[e].wait_recv()
         share(gh, 1 + e, 4 + e + c, 2)
@@ -189,51 +218,32 @@
     settle(gl.at[pl.ds(0, 3), :, pl.ds(0, 3)], ssem.at[8])
 
 
-def stack_kernel(gl, gh, lhs, rci, out, stage, sems):
-    mine = rci[...]
-
-    def held(k):
-        even = jnp.where(k == 0, 0, jnp.where(k == 8, 1, 1 + k // 2))
-        return jnp.where(k % 2 == 0, even, 5 + k // 2)
-
-    def to_out(k):
-        return pltpu.make_async_copy(stage.at[k], out.at[:, k], sems.at[k])
-
-    @pl.loop(0, HOPS, unroll=3)
+def stack_kernel(gl, gh, lhs, rci, ready, out, stage, sems):
+    def to_out(src, k):
+        return pltpu.make_async_copy(src, out.at[:, k], sems.at[k])
+
+    early = [to_out(ready.at[n], 8 * n) for n in (0, 1)]
+    for copy in early:
+        copy.start()
+
+    @pl.loop(1, HOPS - 1, unroll=True)
     def _(k):
-        def tiles(odd):
-            pieces = [(n, at) for n in (0, 1) for at in (2 * odd, 2 * odd + 1)]
-            right = [half[(held(k),) + piece] for piece in pieces for half in (gl, gh)]
-            result = lax.dot_general(
-                lhs[odd],
-                jnp.concatenate(right, axis=0),
-                (((1,), (1,)), ((), ())),
-                preferred_element_type=jnp.float32,
-            )
-            recip = 1.0 / result[0:1]
-            halves = (slice(0, 128), slice(128, 256))
-            return [
-                (result[SEL:, lanes] * jnp.maximum(mine, recip[:, lanes])).reshape(WIDTH, 8, 128)
-                for lanes in halves
-            ]
-
-        lower = lax.broadcasted_iota(jnp.int32, (WIDTH, 8, 128), 1) < BINS
-        for n, (even, odd) in enumerate(zip(tiles(0), tiles(1))):
-            rows = pl.ds(8 * n, 8)
-            stage[k, :, 0, rows] = jnp.where(lower, even, odd)
-            stage[k, :, 1, rows] = pltpu.roll(jnp.where(lower, odd, even), BINS, 1)
-        to_out(k).start()
-
-    @pl.loop(0, HOPS)
+        one_hop(gl, gh, jnp.where(k % 2 == 0, 1 + k // 2, 5 + k // 2), lhs, rci, stage.at[k - 1])
+        to_out(stage.at[k - 1], k).start()
+
+    for copy in early:
+        copy.wait()
+
+    @pl.loop(1, HOPS - 1)
     def _(k):
-        to_out(k).wait()
+        to_out(stage.at[k - 1], k).wait()
 
 
 def per_device(spectra, counts):
     spec = spectra.reshape(USED, WIDTH)
     vmem = pl.BlockSpec(memory_space=pltpu.VMEM)
     hbm = pl.BlockSpec(memory_space=pltpu.HBM)
-    gl, gh, lhs, rci = pl.pallas_call(
+    gl, gh, lhs, rci, ready = pl.pallas_call(
         gather_kernel,
         name="whiten_gather",
         out_shape=(
@@ -241,9 +251,10 @@
             jax.ShapeDtypeStruct((HOPS, 2, 4, HALF, COLS), jnp.bfloat16),
             jax.ShapeDtypeStruct((2, SEL + WIDTH * 8, COLS), jnp.bfloat16),
             jax.ShapeDtypeStruct((WIDTH * 8, 128), jnp.float32),
+            jax.ShapeDtypeStruct((2, WIDTH, 2, 4 * BINS, 128), jnp.float32),
         ),
         in_specs=[hbm, hbm],
-        out_specs=(vmem,) * 4,
+        out_specs=(vmem,) * 5,
         scratch_shapes=[
             pltpu.VMEM((USED, WIDTH), jnp.float32),
             pltpu.VMEM((1, WIDTH), jnp.int32),
@@ -260,10 +271,10 @@
         stack_kernel,
         name="stack",
         out_shape=jax.ShapeDtypeStruct((WIDTH, HOPS, 2, 4 * BINS, 128), jnp.float32),
-        in_specs=[vmem] * 4,
+        in_specs=[vmem] * 5,
         out_specs=hbm,
         scratch_shapes=[
-            pltpu.VMEM((HOPS, WIDTH, 2, 4 * BINS, 128), jnp.float32),
+            pltpu.VMEM((HOPS - 2, WIDTH, 2, 4 * BINS, 128), jnp.float32),
             pltpu.SemaphoreType.DMA((HOPS,)),
         ],
         compiler_params=pltpu.CompilerParams(vmem_limit_bytes=24 * 2**20),
@@ -272,7 +283,7 @@
             bytes_accessed=HOPS * 512 * (COLS * 2 + WIDTH * 8 * 4),
             transcendentals=0,
         ),
-    )(gl, gh, lhs, rci)
+    )(gl, gh, lhs, rci, ready)
     out = out.reshape(WIDTH, HOPS, 2, 4, BINS, 128).swapaxes(3, 4)
     return out.reshape(1, WIDTH, HOPS, 2, BINS, 512)
 

time: 27.6 us -> 27.2 us (0.986)
  Pallas kernels: 27.4 us -> 27.1 us
    pallas_call x1, Pallas kernels: 4.06 us -> 3.71 us  [per_device(): pl.pallas_call(stack_kernel, name='stack', out_shape=jax.ShapeDtypeStruct...]
where the time goes in v1:
time: 27.2 us; the launch traced here: 27.1 us
  Pallas kernels  27.1 us (100%)
    pallas_call x1, Pallas kernels, per_device(): pl.pallas_call(gather_kernel, name='whiten_gather', out_shape=(jax.ShapeD...  23.4 us
    pallas_call x1, Pallas kernels, per_device(): pl.pallas_call(stack_kernel, name='stack', out_shape=jax.ShapeDtypeStruct...  3.71 us

profile of v1, /device:TPU:1, one launch (start us, length us, event | category | flops | bytes accessed | tf_op | source)
XLA Modules:
  0.0 27.1 jit_solution(3171722366456897389)
XLA Ops:
  0.0 23.4 %whiten_gather.1 = (bf16[9,2,4,32,256]{4,3,2,1,0:T(8,128)(2,1)S(1)}, bf16[9,2,4,32,256]{4,3,2,1,0:T(8,128)(2,1)S(1)}, bf16[2,528,256]{2,1,0:T(8,128)(2,1)S(1)}, ...) custom-call(f32[240,64]{1,0:T(8,128)} %bitcast.6, s32[1,64]{1,0:T(1,128)} %cnt_in.1), custom_call_target="tpu_custom_call" | custom-call | tf_op jit(solution)/shard_map/whiten_gather/pallas_call | solution.py:246
  23.4 3.7 %stack.1 = f32[64,9,2,16,128]{4,3,2,1,0:T(8,128)} custom-call(bf16[9,2,4,32,256]{4,3,2,1,0:T(8,128)(2,1)S(1)} %get-tuple-element.10.gl, bf16[9,2,4,32,256]{4,3,2,1,0:T(8,128)(2,1)S(1)} %get-tuple-element.11.gh, bf16[2,528,256]{2,1,0:T(8,128)(2,1)S(1)} %get-tuple-element.12.lhs, f32[512,128]{1,0:T(8,128)S(1)} %get-tuple-element.13.rci, ...), custom_call_target="tpu_custom_call" | custom-call | flops 1245708288 | bytes 11796480 | tf_op jit(solution)/shard_map/stack/pallas_call | solution.py:270

commit v2 on v1

--- a/solution.py
+++ b/solution.py
@@ -156,11 +156,11 @@
     for copy in local:
         copy.wait()
 
-    def share(half, index, to, send):
-        remote(half.at[index], half.at[to], sibling, send, SHARED + send)
+    def share(half, index, to, send, recv=SHARED):
+        remote(half.at[index], half.at[to], sibling, send, recv + send)
 
     def share_end(half, send):
-        share(half, 1 - c, 8 - 3 * c, send)
+        share(half, 1 - c, 8 - 3 * c, send, SHARED + 2)
 
     def x_copies(blocks, send, recv):
         column = gl.at[blocks, :, x]
@@ -168,12 +168,12 @@
 
     taken = {e: jnp.where((z + 4 - e) % 4 > z, 1, 0) for e in (3, 2, 1)}
 
+    settle(gl.at[0, 0, pl.ds(0, 3)], rsem.at[1])
+    for e in taken:
+        remote(gl.at[taken[e], :, x], gl.at[1 + e, :, x], along_z(-e), 5, 3)
     settle(gh.at[0, 0, pl.ds(0, 3)], rsem.at[0])
     for four_on, rel in y_steps:
         remote(gh.at[0, ylo], gh.at[four_on, ylo], along_y(four_on, rel), 4, 2 + 10 * four_on)
-    settle(gl.at[0, 0, pl.ds(0, 3)], rsem.at[1])
-    for e in taken:
-        remote(gl.at[taken[e], :, x], gl.at[1 + e, :, x], along_z(-e), 5, 3)
     z_copies = {
         e: plan(gh.at[taken[e]], gh.at[1 + e], along_z(-e), 7, 12 + e) for e in taken
     }
@@ -182,19 +182,22 @@
     for e in taken:
         pl.when(taken[e] == 0)(z_copies[e].start)
     near = x_copies(pl.ds(0, 2), 6, 4)
-    settle(gh.at[0], rsem.at[12])
-    for e in taken:
-        pl.when(taken[e] == 1)(z_copies[e].start)
-    share_end(gh, 2)
     settle(gl.at[0, pl.ds(0, 2), pl.ds(0, 3)], rsem.at[3])
     rest = pl.ds(2, 3)
     beyond = x_copies(rest, 8, 8)
+    settle(gh.at[0], rsem.at[12])
+    for e in taken:
+        pl.when(taken[e] == 1)(z_copies[e].start)
+    share_end(gh, 2)
     for i in steps:
         near[i].wait_recv()
     share_end(gl, 3)
 
     for n in (0, 1):
         one_hop(gl, gh, n, lhs, rci, ready.at[n])
+    settle(gh.at[0], rsem.at[SHARED + 4])
+    settle(gl.at[0], rsem.at[SHARED + 5])
+    one_hop(gl, gh, 5 + 3 * c, lhs, rci, ready.at[2])
 
     for e in taken:
         z_copies[e].wait_recv()
@@ -205,8 +208,8 @@
         at = (x + 4 - i) % 4
         share(gl, (rest, every, at), (pl.ds(5 + c, 3), every, at), 3)
 
-    settle(gh.at[pl.ds(5, 4)], rsem.at[SHARED + 2])
-    settle(gl.at[pl.ds(5, 4)], rsem.at[SHARED + 3])
+    settle(gh.at[pl.ds(5, 3)], rsem.at[SHARED + 2])
+    settle(gl.at[pl.ds(5, 3)], rsem.at[SHARED + 3])
     settle(gh.at[0, 0, pl.ds(0, 3)], ssem.at[0])
     settle(gl.at[0, 0, pl.ds(0, 3)], ssem.at[1])
     settle(gh.at[pl.ds(5, 4)], ssem.at[2])
@@ -222,21 +225,18 @@
     def to_out(src, k):
         return pltpu.make_async_copy(src, out.at[:, k], sems.at[k])
 
-    early = [to_out(ready.at[n], 8 * n) for n in (0, 1)]
+    c = lax.axis_index("col") % 2
+    early = [to_out(ready.at[n], k) for n, k in enumerate((0, HOPS - 1, 1 + 6 * c))]
     for copy in early:
         copy.start()
-
-    @pl.loop(1, HOPS - 1, unroll=True)
-    def _(k):
-        one_hop(gl, gh, jnp.where(k % 2 == 0, 1 + k // 2, 5 + k // 2), lhs, rci, stage.at[k - 1])
-        to_out(stage.at[k - 1], k).start()
-
-    for copy in early:
+    later = [2 - c + n for n in range(HOPS - 3)]
+    copies = [to_out(stage.at[n], k) for n, k in enumerate(later)]
+    for n, k in enumerate(later):
+        held = jnp.where(k % 2 == 0, 1 + k // 2, 5 + k // 2)
+        one_hop(gl, gh, held, lhs, rci, stage.at[n])
+        copies[n].start()
+    for copy in early + copies:
         copy.wait()
-
-    @pl.loop(1, HOPS - 1)
-    def _(k):
-        to_out(stage.at[k - 1], k).wait()
 
 
 def per_device(spectra, counts):
@@ -251,7 +251,7 @@
             jax.ShapeDtypeStruct((HOPS, 2, 4, HALF, COLS), jnp.bfloat16),
             jax.ShapeDtypeStruct((2, SEL + WIDTH * 8, COLS), jnp.bfloat16),
             jax.ShapeDtypeStruct((WIDTH * 8, 128), jnp.float32),
-            jax.ShapeDtypeStruct((2, WIDTH, 2, 4 * BINS, 128), jnp.float32),
+            jax.ShapeDtypeStruct((3, WIDTH, 2, 4 * BINS, 128), jnp.float32),
         ),
         in_specs=[hbm, hbm],
         out_specs=(vmem,) * 5,
@@ -260,7 +260,7 @@
             pltpu.VMEM((1, WIDTH), jnp.int32),
             pltpu.VMEM((WIDTH, COLS), jnp.bfloat16),
             pltpu.SemaphoreType.DMA((9,)),
-            pltpu.SemaphoreType.DMA((SHARED + 4,)),
+            pltpu.SemaphoreType.DMA((SHARED + 6,)),
             pltpu.SemaphoreType.DMA((4,)),
         ],
         compiler_params=pltpu.CompilerParams(
@@ -274,7 +274,7 @@
         in_specs=[vmem] * 5,
         out_specs=hbm,
         scratch_shapes=[
-            pltpu.VMEM((HOPS - 2, WIDTH, 2, 4 * BINS, 128), jnp.float32),
+            pltpu.VMEM((HOPS - 3, WIDTH, 2, 4 * BINS, 128), jnp.float32),
             pltpu.SemaphoreType.DMA((HOPS,)),
         ],
         compiler_params=pltpu.CompilerParams(vmem_limit_bytes=24 * 2**20),

time: 27.2 us -> 27.5 us (1.011)
  Pallas kernels: 27.1 us -> 27.4 us
where the time goes in v2:
time: 27.5 us; the launch traced here: 27.4 us
  Pallas kernels  27.4 us (100%)
    pallas_call x1, Pallas kernels, per_device(): pl.pallas_call(gather_kernel, name='whiten_gather', out_shape=(jax.ShapeD...  23.5 us
    pallas_call x1, Pallas kernels, per_device(): pl.pallas_call(stack_kernel, name='stack', out_shape=jax.ShapeDtypeStruct...  3.82 us

profile of v2, /device:TPU:1, one launch (start us, length us, event | category | flops | bytes accessed | tf_op | source)
XLA Modules:
  0.0 27.4 jit_solution(7103438549608124208)
XLA Ops:
  0.0 23.5 %whiten_gather.1 = (bf16[9,2,4,32,256]{4,3,2,1,0:T(8,128)(2,1)S(1)}, bf16[9,2,4,32,256]{4,3,2,1,0:T(8,128)(2,1)S(1)}, bf16[2,528,256]{2,1,0:T(8,128)(2,1)S(1)}, ...) custom-call(f32[240,64]{1,0:T(8,128)} %bitcast.6, s32[1,64]{1,0:T(1,128)} %cnt_in.1), custom_call_target="tpu_custom_call" | custom-call | tf_op jit(solution)/shard_map/whiten_gather/pallas_call | solution.py:246
  23.5 3.8 %stack.1 = f32[64,9,2,16,128]{4,3,2,1,0:T(8,128)} custom-call(bf16[9,2,4,32,256]{4,3,2,1,0:T(8,128)(2,1)S(1)} %get-tuple-element.10.gl, bf16[9,2,4,32,256]{4,3,2,1,0:T(8,128)(2,1)S(1)} %get-tuple-element.11.gh, bf16[2,528,256]{2,1,0:T(8,128)(2,1)S(1)} %get-tuple-element.12.lhs, f32[512,128]{1,0:T(8,128)S(1)} %get-tuple-element.13.rci, ...), custom_call_target="tpu_custom_call" | custom-call | flops 1245708288 | bytes 11796480 | tf_op jit(solution)/shard_map/stack/pallas_call | solution.py:270

commit v3 on v1

--- a/solution.py
+++ b/solution.py
@@ -159,8 +159,11 @@
     def share(half, index, to, send):
         remote(half.at[index], half.at[to], sibling, send, SHARED + send)
 
-    def share_end(half, send):
-        share(half, 1 - c, 8 - 3 * c, send)
+    def share_column(i):
+        at = (x + 4 - i) % 4
+        share(gl, (rest, every, at), (pl.ds(5 + c, 3), every, at), 3)
+
+    rest = pl.ds(2, 3)
 
     def x_copies(blocks, send, recv):
         column = gl.at[blocks, :, x]
@@ -168,9 +171,16 @@
 
     taken = {e: jnp.where((z + 4 - e) % 4 > z, 1, 0) for e in (3, 2, 1)}
 
+    def share_row(rel):
+        @pl.when(c == 1)
+        def _():
+            row = across if rel else ylo
+            share(gh, (0, row), (5, row), 2)
+
     settle(gh.at[0, 0, pl.ds(0, 3)], rsem.at[0])
     for four_on, rel in y_steps:
         remote(gh.at[0, ylo], gh.at[four_on, ylo], along_y(four_on, rel), 4, 2 + 10 * four_on)
+    share_row(0)
     settle(gl.at[0, 0, pl.ds(0, 3)], rsem.at[1])
     for e in taken:
         remote(gl.at[taken[e], :, x], gl.at[1 + e, :, x], along_z(-e), 5, 3)
@@ -181,29 +191,28 @@
     settle(gh.at[0, 0], rsem.at[2])
     for e in taken:
         pl.when(taken[e] == 0)(z_copies[e].start)
+    share_row(1)
     near = x_copies(pl.ds(0, 2), 6, 4)
     settle(gh.at[0], rsem.at[12])
     for e in taken:
         pl.when(taken[e] == 1)(z_copies[e].start)
-    share_end(gh, 2)
+    pl.when(c == 0)(lambda: share(gh, 1, 8, 2))
     settle(gl.at[0, pl.ds(0, 2), pl.ds(0, 3)], rsem.at[3])
-    rest = pl.ds(2, 3)
+    share_column(0)
     beyond = x_copies(rest, 8, 8)
     for i in steps:
         near[i].wait_recv()
-    share_end(gl, 3)
+    share(gl, 1 - c, 8 - 3 * c, 3)
 
     for n in (0, 1):
         one_hop(gl, gh, n, lhs, rci, ready.at[n])
 
-    for e in taken:
+    for e in (1, 2, 3):
         z_copies[e].wait_recv()
         share(gh, 1 + e, 4 + e + c, 2)
-    for i in (0,) + steps:
-        if i:
-            beyond[i].wait_recv()
-        at = (x + 4 - i) % 4
-        share(gl, (rest, every, at), (pl.ds(5 + c, 3), every, at), 3)
+    for i in steps:
+        beyond[i].wait_recv()
+        share_column(i)
 
     settle(gh.at[pl.ds(5, 4)], rsem.at[SHARED + 2])
     settle(gl.at[pl.ds(5, 4)], rsem.at[SHARED + 3])

time: 27.2 us -> 27.2 us (level)
  no operation moved by 1% of the time
where the time goes in v3:
time: 27.2 us; the launch traced here: 27.1 us
  Pallas kernels  27.1 us (100%)
    pallas_call x1, Pallas kernels, per_device(): pl.pallas_call(gather_kernel, name='whiten_gather', out_shape=(jax.ShapeD...  23.4 us
    pallas_call x1, Pallas kernels, per_device(): pl.pallas_call(stack_kernel, name='stack', out_shape=jax.ShapeDtypeStruct...  3.71 us

profile of v3, /device:TPU:1, one launch (start us, length us, event | category | flops | bytes accessed | tf_op | source)
XLA Modules:
  0.0 27.1 jit_solution(11650938683049612647)
XLA Ops:
  0.0 23.4 %whiten_gather.1 = (bf16[9,2,4,32,256]{4,3,2,1,0:T(8,128)(2,1)S(1)}, bf16[9,2,4,32,256]{4,3,2,1,0:T(8,128)(2,1)S(1)}, bf16[2,528,256]{2,1,0:T(8,128)(2,1)S(1)}, ...) custom-call(f32[240,64]{1,0:T(8,128)} %bitcast.6, s32[1,64]{1,0:T(1,128)} %cnt_in.1), custom_call_target="tpu_custom_call" | custom-call | tf_op jit(solution)/shard_map/whiten_gather/pallas_call | solution.py:255
  23.4 3.7 %stack.1 = f32[64,9,2,16,128]{4,3,2,1,0:T(8,128)} custom-call(bf16[9,2,4,32,256]{4,3,2,1,0:T(8,128)(2,1)S(1)} %get-tuple-element.10.gl, bf16[9,2,4,32,256]{4,3,2,1,0:T(8,128)(2,1)S(1)} %get-tuple-element.11.gh, bf16[2,528,256]{2,1,0:T(8,128)(2,1)S(1)} %get-tuple-element.12.lhs, f32[512,128]{1,0:T(8,128)S(1)} %get-tuple-element.13.rci, ...), custom_call_target="tpu_custom_call" | custom-call | flops 1245708288 | bytes 11796480 | tf_op jit(solution)/shard_map/stack/pallas_call | solution.py:279

commit v4 on v1

--- a/solution.py
+++ b/solution.py
@@ -53,27 +53,39 @@
     for copy in fetch:
         copy.start()
     r, d = lax.axis_index("row"), lax.axis_index("col")
-    x, ylo = r % 4, r // 4
-    c, q = d % 2, d // 2
-    z, yhi = q % 4, q // 4
-
-    def dev(x_, ylo_, q_, c_):
-        return (ylo_ * 4 + x_, q_ * 2 + c_)
-
-    sibling = dev(x, ylo, q, 1 - c)
+    ylo = jnp.where(r >= 4, 1, 0)
+    x = r - 4 * ylo
+    yhi = jnp.where(d >= 8, 1, 0)
+    rest_of_d = d - 8 * yhi
+    z = sum(jnp.where(rest_of_d >= n, 1, 0) for n in (2, 4, 6))
+    c = rest_of_d - 2 * z
+
+    def wrap(n):
+        return jnp.where(n >= 4, n - 4, n)
+
+    def dev(x_, ylo_, yhi_, z_, c_):
+        return (ylo_ * 4 + x_, yhi_ * 8 + z_ * 2 + c_)
+
+    sibling = dev(x, ylo, yhi, z, 1 - c)
     across = 1 - ylo
 
     steps = (2, 1, 3)
     y_steps = ((0, 1), (1, 1), (1, 0))
 
+    x_at = {i: wrap(x + i) for i in (1, 2, 3)}
+    x_at[0] = x
+    x_dev = {i: dev(x_at[i], ylo, yhi, z, c) for i in steps}
+    z_dev = {e: dev(x, ylo, yhi, wrap(z + e), c) for e in steps}
+    y_dev = {at: dev(x, across if at[1] else ylo, 1 - yhi if at[0] else yhi, z, c) for at in y_steps}
+
     def along_x(i):
-        return dev((x + i) % 4, ylo, q, c)
-
-    def along_y(four_on, rel):
-        return dev(x, across if rel else ylo, (q + 4 * four_on) % 8, c)
+        return x_dev[i]
+
+    def along_y(*at):
+        return y_dev[at]
 
     def along_z(e):
-        return dev(x, ylo, yhi * 4 + (z + e) % 4, c)
+        return z_dev[e % 4]
 
     barrier = pltpu.get_barrier_semaphore()
     sources = [along_x(i) for i in steps] + [along_y(*at) for at in y_steps]
@@ -166,7 +178,7 @@
         column = gl.at[blocks, :, x]
         return {i: remote(column, column, along_x(i), send, recv + i) for i in steps}
 
-    taken = {e: jnp.where((z + 4 - e) % 4 > z, 1, 0) for e in (3, 2, 1)}
+    taken = {e: jnp.where(z < e, 1, 0) for e in (3, 2, 1)}
 
     settle(gh.at[0, 0, pl.ds(0, 3)], rsem.at[0])
     for four_on, rel in y_steps:
@@ -202,7 +214,7 @@
     for i in (0,) + steps:
         if i:
             beyond[i].wait_recv()
-        at = (x + 4 - i) % 4
+        at = x_at[-i % 4]
         share(gl, (rest, every, at), (pl.ds(5 + c, 3), every, at), 3)
 
     settle(gh.at[pl.ds(5, 4)], rsem.at[SHARED + 2])

time: 27.2 us -> 27.2 us (level)
  no operation moved by 1% of the time
where the time goes in v4:
time: 27.2 us; the launch traced here: 27.1 us
  Pallas kernels  27.1 us (100%)
    pallas_call x1, Pallas kernels, per_device(): pl.pallas_call(gather_kernel, name='whiten_gather', out_shape=(jax.ShapeD...  23.4 us
    pallas_call x1, Pallas kernels, per_device(): pl.pallas_call(stack_kernel, name='stack', out_shape=jax.ShapeDtypeStruct...  3.71 us

profile of v4, /device:TPU:1, one launch (start us, length us, event | category | flops | bytes accessed | tf_op | source)
XLA Modules:
  0.0 27.1 jit_solution(16866503385718624778)
XLA Ops:
  0.0 23.4 %whiten_gather.1 = (bf16[9,2,4,32,256]{4,3,2,1,0:T(8,128)(2,1)S(1)}, bf16[9,2,4,32,256]{4,3,2,1,0:T(8,128)(2,1)S(1)}, bf16[2,528,256]{2,1,0:T(8,128)(2,1)S(1)}, ...) custom-call(f32[240,64]{1,0:T(8,128)} %bitcast.6, s32[1,64]{1,0:T(1,128)} %cnt_in.1), custom_call_target="tpu_custom_call" | custom-call | tf_op jit(solution)/shard_map/whiten_gather/pallas_call | solution.py:258
  23.4 3.7 %stack.1 = f32[64,9,2,16,128]{4,3,2,1,0:T(8,128)} custom-call(bf16[9,2,4,32,256]{4,3,2,1,0:T(8,128)(2,1)S(1)} %get-tuple-element.10.gl, bf16[9,2,4,32,256]{4,3,2,1,0:T(8,128)(2,1)S(1)} %get-tuple-element.11.gh, bf16[2,528,256]{2,1,0:T(8,128)(2,1)S(1)} %get-tuple-element.12.lhs, f32[512,128]{1,0:T(8,128)S(1)} %get-tuple-element.13.rci, ...), custom_call_target="tpu_custom_call" | custom-call | flops 1245708288 | bytes 11796480 | tf_op jit(solution)/shard_map/stack/pallas_call | solution.py:282

commit v5 on v4

--- a/solution.py
+++ b/solution.py
@@ -180,12 +180,12 @@
 
     taken = {e: jnp.where(z < e, 1, 0) for e in (3, 2, 1)}
 
+    settle(gl.at[0, 0, pl.ds(0, 3)], rsem.at[1])
+    for e in taken:
+        remote(gl.at[taken[e], :, x], gl.at[1 + e, :, x], along_z(-e), 5, 3)
     settle(gh.at[0, 0, pl.ds(0, 3)], rsem.at[0])
     for four_on, rel in y_steps:
         remote(gh.at[0, ylo], gh.at[four_on, ylo], along_y(four_on, rel), 4, 2 + 10 * four_on)
-    settle(gl.at[0, 0, pl.ds(0, 3)], rsem.at[1])
-    for e in taken:
-        remote(gl.at[taken[e], :, x], gl.at[1 + e, :, x], along_z(-e), 5, 3)
     z_copies = {
         e: plan(gh.at[taken[e]], gh.at[1 + e], along_z(-e), 7, 12 + e) for e in taken
     }
@@ -201,6 +201,12 @@
     settle(gl.at[0, pl.ds(0, 2), pl.ds(0, 3)], rsem.at[3])
     rest = pl.ds(2, 3)
     beyond = x_copies(rest, 8, 8)
+
+    def share_column(i):
+        at = x_at[-i % 4]
+        share(gl, (rest, every, at), (pl.ds(5 + c, 3), every, at), 3)
+
+    share_column(0)
     for i in steps:
         near[i].wait_recv()
     share_end(gl, 3)
@@ -208,14 +214,12 @@
     for n in (0, 1):
         one_hop(gl, gh, n, lhs, rci, ready.at[n])
 
-    for e in taken:
+    for e in (1, 2, 3):
         z_copies[e].wait_recv()
         share(gh, 1 + e, 4 + e + c, 2)
-    for i in (0,) + steps:
-        if i:
-            beyond[i].wait_recv()
-        at = x_at[-i % 4]
-        share(gl, (rest, every, at), (pl.ds(5 + c, 3), every, at), 3)
+    for i in steps:
+        beyond[i].wait_recv()
+        share_column(i)
 
     settle(gh.at[pl.ds(5, 4)], rsem.at[SHARED + 2])
     settle(gl.at[pl.ds(5, 4)], rsem.at[SHARED + 3])

time: 27.2 us -> 27.4 us (level)
  no operation moved by 1% of the time
where the time goes in v5:
time: 27.4 us; the launch traced here: 27.3 us
  Pallas kernels  27.3 us (100%)
    pallas_call x1, Pallas kernels, per_device(): pl.pallas_call(gather_kernel, name='whiten_gather', out_shape=(jax.ShapeD...  23.6 us
    pallas_call x1, Pallas kernels, per_device(): pl.pallas_call(stack_kernel, name='stack', out_shape=jax.ShapeDtypeStruct...  3.71 us

profile of v5, /device:TPU:1, one launch (start us, length us, event | category | flops | bytes accessed | tf_op | source)
XLA Modules:
  0.0 27.3 jit_solution(8744150379005576428)
XLA Ops:
  0.0 23.6 %whiten_gather.1 = (bf16[9,2,4,32,256]{4,3,2,1,0:T(8,128)(2,1)S(1)}, bf16[9,2,4,32,256]{4,3,2,1,0:T(8,128)(2,1)S(1)}, bf16[2,528,256]{2,1,0:T(8,128)(2,1)S(1)}, ...) custom-call(f32[240,64]{1,0:T(8,128)} %bitcast.6, s32[1,64]{1,0:T(1,128)} %cnt_in.1), custom_call_target="tpu_custom_call" | custom-call | tf_op jit(solution)/shard_map/whiten_gather/pallas_call | solution.py:262
  23.6 3.7 %stack.1 = f32[64,9,2,16,128]{4,3,2,1,0:T(8,128)} custom-call(bf16[9,2,4,32,256]{4,3,2,1,0:T(8,128)(2,1)S(1)} %get-tuple-element.10.gl, bf16[9,2,4,32,256]{4,3,2,1,0:T(8,128)(2,1)S(1)} %get-tuple-element.11.gh, bf16[2,528,256]{2,1,0:T(8,128)(2,1)S(1)} %get-tuple-element.12.lhs, f32[512,128]{1,0:T(8,128)S(1)} %get-tuple-element.13.rci, ...), custom_call_target="tpu_custom_call" | custom-call | flops 1245708288 | bytes 11796480 | tf_op jit(solution)/shard_map/stack/pallas_call | solution.py:286

commit v6 on v4

--- a/solution.py
+++ b/solution.py
@@ -168,11 +168,11 @@
     for copy in local:
         copy.wait()
 
-    def share(half, index, to, send):
-        remote(half.at[index], half.at[to], sibling, send, SHARED + send)
+    def share(half, index, to, send, recv=SHARED):
+        remote(half.at[index], half.at[to], sibling, send, recv + send)
 
     def share_end(half, send):
-        share(half, 1 - c, 8 - 3 * c, send)
+        share(half, 1 - c, 8 - 3 * c, send, SHARED + 2)
 
     def x_copies(blocks, send, recv):
         column = gl.at[blocks, :, x]
@@ -217,8 +217,11 @@
         at = x_at[-i % 4]
         share(gl, (rest, every, at), (pl.ds(5 + c, 3), every, at), 3)
 
-    settle(gh.at[pl.ds(5, 4)], rsem.at[SHARED + 2])
-    settle(gl.at[pl.ds(5, 4)], rsem.at[SHARED + 3])
+    settle(gh.at[0], rsem.at[SHARED + 4])
+    settle(gl.at[0], rsem.at[SHARED + 5])
+    one_hop(gl, gh, 5 + 3 * c, lhs, rci, ready.at[2])
+    settle(gh.at[pl.ds(5, 3)], rsem.at[SHARED + 2])
+    settle(gl.at[pl.ds(5, 3)], rsem.at[SHARED + 3])
     settle(gh.at[0, 0, pl.ds(0, 3)], ssem.at[0])
     settle(gl.at[0, 0, pl.ds(0, 3)], ssem.at[1])
     settle(gh.at[pl.ds(5, 4)], ssem.at[2])
@@ -234,21 +237,17 @@
     def to_out(src, k):
         return pltpu.make_async_copy(src, out.at[:, k], sems.at[k])
 
-    early = [to_out(ready.at[n], 8 * n) for n in (0, 1)]
+    c = lax.axis_index("col") % 2
+    early = [to_out(ready.at[n], k) for n, k in enumerate((0, HOPS - 1, 1 + 6 * c))]
     for copy in early:
         copy.start()
-
-    @pl.loop(1, HOPS - 1, unroll=True)
-    def _(k):
-        one_hop(gl, gh, jnp.where(k % 2 == 0, 1 + k // 2, 5 + k // 2), lhs, rci, stage.at[k - 1])
-        to_out(stage.at[k - 1], k).start()
-
-    for copy in early:
+    places = [(7 - 6 * c, 8 - 3 * c), (2, 2), (3, 6), (4, 3), (5, 7), (6, 4)]
+    copies = [to_out(stage.at[n], k) for n, (k, held) in enumerate(places)]
+    for n, (k, held) in enumerate(places):
+        one_hop(gl, gh, held, lhs, rci, stage.at[n])
+        copies[n].start()
+    for copy in early + copies:
         copy.wait()
-
-    @pl.loop(1, HOPS - 1)
-    def _(k):
-        to_out(stage.at[k - 1], k).wait()
 
 
 def per_device(spectra, counts):
@@ -263,7 +262,7 @@
             jax.ShapeDtypeStruct((HOPS, 2, 4, HALF, COLS), jnp.bfloat16),
             jax.ShapeDtypeStruct((2, SEL + WIDTH * 8, COLS), jnp.bfloat16),
             jax.ShapeDtypeStruct((WIDTH * 8, 128), jnp.float32),
-            jax.ShapeDtypeStruct((2, WIDTH, 2, 4 * BINS, 128), jnp.float32),
+            jax.ShapeDtypeStruct((3, WIDTH, 2, 4 * BINS, 128), jnp.float32),
         ),
         in_specs=[hbm, hbm],
         out_specs=(vmem,) * 5,
@@ -272,7 +271,7 @@
             pltpu.VMEM((1, WIDTH), jnp.int32),
             pltpu.VMEM((WIDTH, COLS), jnp.bfloat16),
             pltpu.SemaphoreType.DMA((9,)),
-            pltpu.SemaphoreType.DMA((SHARED + 4,)),
+            pltpu.SemaphoreType.DMA((SHARED + 6,)),
             pltpu.SemaphoreType.DMA((4,)),
         ],
         compiler_params=pltpu.CompilerParams(
@@ -286,7 +285,7 @@
         in_specs=[vmem] * 5,
         out_specs=hbm,
         scratch_shapes=[
-            pltpu.VMEM((HOPS - 2, WIDTH, 2, 4 * BINS, 128), jnp.float32),
+            pltpu.VMEM((HOPS - 3, WIDTH, 2, 4 * BINS, 128), jnp.float32),
             pltpu.SemaphoreType.DMA((HOPS,)),
         ],
         compiler_params=pltpu.CompilerParams(vmem_limit_bytes=24 * 2**20),

time: 27.2 us -> 27.2 us (level)
  no operation moved by 1% of the time
where the time goes in v6:
time: 27.2 us; the launch traced here: 27.1 us
  Pallas kernels  27.1 us (100%)
    pallas_call x1, Pallas kernels, per_device(): pl.pallas_call(gather_kernel, name='whiten_gather', out_shape=(jax.ShapeD...  23.4 us
    pallas_call x1, Pallas kernels, per_device(): pl.pallas_call(stack_kernel, name='stack', out_shape=jax.ShapeDtypeStruct...  3.7 us

profile of v6, /device:TPU:1, one launch (start us, length us, event | category | flops | bytes accessed | tf_op | source)
XLA Modules:
  0.0 27.1 jit_solution(17116940311489777849)
XLA Ops:
  0.0 23.4 %whiten_gather.1 = (bf16[9,2,4,32,256]{4,3,2,1,0:T(8,128)(2,1)S(1)}, bf16[9,2,4,32,256]{4,3,2,1,0:T(8,128)(2,1)S(1)}, bf16[2,528,256]{2,1,0:T(8,128)(2,1)S(1)}, ...) custom-call(f32[240,64]{1,0:T(8,128)} %bitcast.6, s32[1,64]{1,0:T(1,128)} %cnt_in.1), custom_call_target="tpu_custom_call" | custom-call | tf_op jit(solution)/shard_map/whiten_gather/pallas_call | solution.py:257
  23.4 3.7 %stack.1 = f32[64,9,2,16,128]{4,3,2,1,0:T(8,128)} custom-call(bf16[9,2,4,32,256]{4,3,2,1,0:T(8,128)(2,1)S(1)} %get-tuple-element.10.gl, bf16[9,2,4,32,256]{4,3,2,1,0:T(8,128)(2,1)S(1)} %get-tuple-element.11.gh, bf16[2,528,256]{2,1,0:T(8,128)(2,1)S(1)} %get-tuple-element.12.lhs, f32[512,128]{1,0:T(8,128)S(1)} %get-tuple-element.13.rci, ...), custom_call_target="tpu_custom_call" | custom-call | flops 1245708288 | bytes 11796480 | tf_op jit(solution)/shard_map/stack/pallas_call | solution.py:281

commit v7 on v4

--- a/solution.py
+++ b/solution.py
@@ -180,12 +180,17 @@
 
     taken = {e: jnp.where(z < e, 1, 0) for e in (3, 2, 1)}
 
+    def y_send(at):
+        four_on = at[0]
+        remote(gh.at[0, ylo], gh.at[four_on, ylo], along_y(*at), 4, 2 + 10 * four_on)
+
     settle(gh.at[0, 0, pl.ds(0, 3)], rsem.at[0])
-    for four_on, rel in y_steps:
-        remote(gh.at[0, ylo], gh.at[four_on, ylo], along_y(four_on, rel), 4, 2 + 10 * four_on)
+    y_send(y_steps[0])
     settle(gl.at[0, 0, pl.ds(0, 3)], rsem.at[1])
     for e in taken:
         remote(gl.at[taken[e], :, x], gl.at[1 + e, :, x], along_z(-e), 5, 3)
+    for at in y_steps[1:]:
+        y_send(at)
     z_copies = {
         e: plan(gh.at[taken[e]], gh.at[1 + e], along_z(-e), 7, 12 + e) for e in taken
     }

time: 27.2 us -> 27.2 us (level)
  no operation moved by 1% of the time
where the time goes in v7:
time: 27.2 us; the launch traced here: 27.1 us
  Pallas kernels  27.1 us (100%)
    pallas_call x1, Pallas kernels, per_device(): pl.pallas_call(gather_kernel, name='whiten_gather', out_shape=(jax.ShapeD...  23.4 us
    pallas_call x1, Pallas kernels, per_device(): pl.pallas_call(stack_kernel, name='stack', out_shape=jax.ShapeDtypeStruct...  3.71 us

profile of v7, /device:TPU:1, one launch (start us, length us, event | category | flops | bytes accessed | tf_op | source)
XLA Modules:
  0.0 27.1 jit_solution(3070794314105091530)
XLA Ops:
  0.0 23.4 %whiten_gather.1 = (bf16[9,2,4,32,256]{4,3,2,1,0:T(8,128)(2,1)S(1)}, bf16[9,2,4,32,256]{4,3,2,1,0:T(8,128)(2,1)S(1)}, bf16[2,528,256]{2,1,0:T(8,128)(2,1)S(1)}, ...) custom-call(f32[240,64]{1,0:T(8,128)} %bitcast.6, s32[1,64]{1,0:T(1,128)} %cnt_in.1), custom_call_target="tpu_custom_call" | custom-call | tf_op jit(solution)/shard_map/whiten_gather/pallas_call | solution.py:263
  23.4 3.7 %stack.1 = f32[64,9,2,16,128]{4,3,2,1,0:T(8,128)} custom-call(bf16[9,2,4,32,256]{4,3,2,1,0:T(8,128)(2,1)S(1)} %get-tuple-element.10.gl, bf16[9,2,4,32,256]{4,3,2,1,0:T(8,128)(2,1)S(1)} %get-tuple-element.11.gh, bf16[2,528,256]{2,1,0:T(8,128)(2,1)S(1)} %get-tuple-element.12.lhs, f32[512,128]{1,0:T(8,128)S(1)} %get-tuple-element.13.rci, ...), custom_call_target="tpu_custom_call" | custom-call | flops 1245708288 | bytes 11796480 | tf_op jit(solution)/shard_map/stack/pallas_call | solution.py:287
